TPU v7x, 32 devices: a whole 2x2x4 slice. The times are simulated.
32 devices in a mesh: parts: 2 (over x), store: 4 (over z), tensor: 4 (over y, core).
Axes of the slice: x: 2, y: 2, z: 4, core: 2. Of those that a mesh axis runs over, the one named last changes fastest.
Arguments:
- tokens: bfloat16 [4096, 8192], P(('parts', 'store'), 'tensor'), parts along dimension 0, may hold values from -6 to 6
- output_weight: bfloat16 [8192, 8192], P('tensor'), may hold values from -0.0625 to 0.0625
- adapter_down_maps: bfloat16 [48, 64, 8192], P('store', None, 'tensor'), may hold values from -0.0625 to 0.0625
- adapter_up_maps: bfloat16 [48, 64, 8192], P('store', None, 'tensor'), may hold values from -0.75 to 0.75
- row_adapter_index: int32 [4096], P(('parts', 'store')), parts along dimension 0, may hold values from 0 to 47, as said below
- store_row_index: int32 [96], P('parts'), parts along dimension 0, may hold values from 0 to 47, as said below
Outputs:
- mixed: bfloat16 [4096, 8192], P(('parts', 'store'), 'tensor'), parts along dimension 0
There are 2 independent parts, one for each index of `parts`. A program takes and returns all parts, laid end to end along the dimension named above; an argument that names none is the same for every part. Nothing has to cross between parts.
Inputs may be any that keep to these rules, and one draw needn't show every extreme that they name: `row_adapter_index`: the rows of one store group use at most 4 distinct adapters held by any one store owner, and exactly 4 of some owner in every group; every group uses adapters of every owner. `store_row_index`: A permutation.
All inputs are finite; a program needn't handle non-finite values.
Results may differ from a plain program's by a relative error of at most 0.0047.
Values may be sent and summed in bfloat16 or wider, within the bound.
A program may use at most 192 MiB of HBM per device.

v0:
```python
import jax
import jax.numpy as jnp
from jax import lax
from jax.sharding import PartitionSpec as P

SLOTS = 4


adapter_scale = 2.0


def on_device(
    tokens, output_weight, adapter_down_maps, adapter_up_maps, row_adapter_index, store_row_index
):
    owners = lax.axis_size("store")
    here = lax.axis_index("store")
    resident_count = adapter_down_maps.shape[0]
    rank_width = adapter_down_maps.shape[1]
    hidden_width = adapter_down_maps.shape[2]
    row_count = tokens.shape[0]
    total = store_row_index.shape[0]
    slot_ids = jnp.arange(total, dtype=jnp.int32)

    def slots_of(ids):
        hits = (ids[:, None] == slot_ids[None, :]).astype(jnp.int32)
        return jnp.sum(hits * store_row_index[None, :], axis=1)

    own_slots = slots_of(row_adapter_index)
    all_ids = lax.all_gather(row_adapter_index, "store", axis=0, tiled=True)
    all_slots = slots_of(all_ids).reshape(owners, row_count)
    held = here * resident_count + jnp.arange(resident_count, dtype=jnp.int32)
    used = jnp.any(all_slots[:, :, None] == held[None, None, :], axis=1)
    place = jnp.cumsum(used.astype(jnp.int32), axis=1) - 1
    capacity = SLOTS
    selector_mask = used[:, None, :] & (place[:, None, :] == jnp.arange(capacity)[None, :, None])
    selector_mask = selector_mask.astype(jnp.bfloat16)
    outgoing_down = jnp.einsum(
        "pon,nwa->powa", selector_mask, adapter_down_maps, preferred_element_type=jnp.float32
    ).astype(jnp.bfloat16)
    outgoing_up = jnp.einsum(
        "pon,nwa->powa", selector_mask, adapter_up_maps, preferred_element_type=jnp.float32
    ).astype(jnp.bfloat16)
    got_a, got_b = (
        lax.all_to_all(outgoing_down, "store", split_axis=0, concat_axis=0, tiled=True),
        lax.all_to_all(outgoing_up, "store", split_axis=0, concat_axis=0, tiled=True),
    )
    whole_a = got_a.reshape(owners * capacity, rank_width, hidden_width)
    whole_b = got_b.reshape(owners * capacity, rank_width, hidden_width)
    own_hits = own_slots[:, None] == slot_ids[None, :]
    own_used = jnp.any(own_hits, axis=0).reshape(owners, resident_count)
    own_place = (jnp.cumsum(own_used.astype(jnp.int32), axis=1) - 1).reshape(total)
    row_place = jnp.sum(own_hits.astype(jnp.int32) * own_place[None, :], axis=1)
    buffer_index = own_slots // resident_count * capacity + row_place
    buffers = owners * capacity
    block_rows = 128
    block_count = (row_count + block_rows - 1) // block_rows + owners * SLOTS
    buffer_ids = jnp.arange(buffers, dtype=jnp.int32)
    member_hits = (buffer_index[:, None] == buffer_ids[None, :]).astype(jnp.int32)
    counts = jnp.sum(member_hits, axis=0)
    spans = (counts + block_rows - 1) // block_rows
    block_start = jnp.cumsum(spans) - spans
    block_end = block_start + spans
    row_start = jnp.cumsum(counts) - counts
    order = jnp.argsort(buffer_index * row_count + jnp.arange(row_count, dtype=jnp.int32))
    block_ids = jnp.arange(block_count, dtype=jnp.int32)
    block_buffer = jnp.sum((block_end[None, :] <= block_ids[:, None]).astype(jnp.int32), axis=1)
    block_buffer = jnp.minimum(block_buffer, buffers - 1)
    live_block = block_ids < jnp.sum(spans)
    in_block = block_ids - block_start[block_buffer]
    position = in_block[:, None] * block_rows + jnp.arange(block_rows, dtype=jnp.int32)[None, :]
    valid = (position < counts[block_buffer][:, None]) & live_block[:, None]
    source = order[jnp.clip(row_start[block_buffer][:, None] + position, 0, row_count - 1)]
    target = jnp.where(valid, source, row_count).reshape(block_count * block_rows)
    block_tokens = tokens[source]
    block_a = whole_a[block_buffer]
    block_down = jnp.einsum(
        "bnf,brf->bnr", block_tokens, block_a, preferred_element_type=jnp.float32
    )
    partial_down = jax.ops.segment_sum(
        block_down.reshape(block_count * block_rows, rank_width), target, num_segments=row_count + 1
    )[:row_count]
    combined_sum = lax.psum(partial_down, "tensor")
    low_rank_state = (adapter_scale * combined_sum).astype(jnp.bfloat16)
    block_low = low_rank_state[source]
    block_b = whole_b[block_buffer]
    block_extra = jnp.einsum("bnr,brf->bnf", block_low, block_b, preferred_element_type=jnp.float32)
    extra = jax.ops.segment_sum(
        block_extra.reshape(block_count * block_rows, hidden_width),
        target,
        num_segments=row_count + 1,
    )[:row_count]
    base_cols = lax.psum_scatter(
        lax.dot_general(
            output_weight, tokens, (((0,), (1,)), ((), ())), preferred_element_type=jnp.float32
        ),
        "tensor",
        scatter_dimension=0,
        tiled=True,
    )
    return (base_cols.T + extra).astype(jnp.bfloat16)


def solution(mesh):
    placed = (
        P(("parts", "store"), "tensor"),
        P("tensor", None),
        P("store", None, "tensor"),
        P("store", None, "tensor"),
        P(("parts", "store")),
        P("parts"),
    )
    return jax.shard_map(
        on_device,
        mesh=mesh,
        in_specs=placed,
        out_specs=P(("parts", "store"), "tensor"),
        check_vma=False,
    )
```

profile of v0, /device:TPU:0, one launch (start us, length us, event | category | flops | bytes accessed | tf_op | source)
XLA Modules:
  0.0 385.8 jit_solution(10001148833458072326)
XLA Ops:
  6.5 13.8 %all-gather = s32[4,1,512]{2,1,0:T(1,128)S(1)} all-gather(s32[1,1,512]{2,1,0:T(1,128)} %bitcast.59), channel_id=1, replica_groups=mesh['parts'=2,'store'=4,'tensor'=4] {'store'}, dimensions={0}, use_global_device_ids=true | all-gather | bytes 10240 | tf_op jit(solution)/shard_map/all_gather | solution.py:29
  20.3 0.8 select_reduce_fusion
  21.8 8.4 %fusion.7 = bf16[4,4,64,2048]{3,1,2,0:T(4,128)(2,1)} fusion(bf16[12,64,2048]{2,1,0:T(8,128)(2,1)} %param.8, s32[4,12]{1,0:T(4,128)S(1)} %copy.41, pred[4,12]{1,0:T(4,128)(4,1)S(1)} %copy.40), kind=kOutput, calls=%fused_computation.18 | convolution fusion | flops 52429184 | bytes 7340272 | tf_op jit(solution)/shard_map/pon,nwa->powa/dot_general | solution.py:37
  30.2 5.0 %all-to-all-start = ((bf16[4,4,64,2048]{3,1,2,0:T(4,128)(2,1)}), bf16[4,4,64,2048]{3,1,2,0:T(4,128)(2,1)}, u32[]{:S(2)}, u32[]{:S(2)}) async-start(bf16[4,4,64,2048]{3,1,2,0:T(4,128)(2,1)} %fusion.7), calls=%async_computation.1 | async-start | bytes 8388608 | tf_op jit(solution)/shard_map/all_to_all | solution.py:44
  36.6 0.7 gather_fusion.1
  37.6 0.7 fusion.28
  38.3 0.7 gather_fusion
  39.0 0.7 gather_fusion.2
  39.7 3.8 sort.17
  43.5 15.4 %gather_fusion.3 = s32[2560]{0:T(1024)S(1)} fusion(s32[512]{0:T(512)S(1)} %get-tuple-element.6, s32[3072]{0:T(1024)S(1)} %pad_clamp_fusion.1), kind=kCustom, calls=%fused_computation.3 | custom fusion | bytes 30720 | tf_op jit(solution)/shard_map/gather | solution.py:72
  59.0 10.8 %gather_fusion.4 = bf16[2560,2048]{1,0:T(8,128)(2,1)} fusion(bf16[512,2048]{1,0:T(8,128)(2,1)S(1)} %copy-done, s32[3072]{0:T(1024)S(1)} %pad_clamp_fusion), kind=kCustom, calls=%fused_computation.4 | custom fusion | bytes 20981760 | tf_op jit(solution)/shard_map/gather | solution.py:74
  69.8 0.6 iota_compare_fusion.6
  70.5 55.5 %all-to-all-done = bf16[4,4,64,2048]{3,1,2,0:T(4,128)(2,1)} async-done(((bf16[4,4,64,2048]{3,1,2,0:T(4,128)(2,1)}), bf16[4,4,64,2048]{3,1,2,0:T(4,128)(2,1)}, u32[]{:S(2)}, u32[]{:S(2)}) %all-to-all-start) | async-done | bytes 4194336 | tf_op jit(solution)/shard_map/all_to_all | solution.py:44
  126.0 6.5 %copy.43 = bf16[4,4,64,2048]{3,2,1,0:T(8,128)(2,1)} copy(bf16[4,4,64,2048]{3,1,2,0:T(4,128)(2,1)} %all-to-all-done) | data formatting | bytes 8388608 | tf_op jit(solution)/shard_map/all_to_all | solution.py:44
  132.5 6.2 %gather_fusion.5 = bf16[20,64,2048]{2,1,0:T(8,128)(2,1)} fusion(bf16[16,64,2048]{2,1,0:T(8,128)(2,1)} %bitcast.55, s32[1024]{0:T(1024)S(1)} %pad_clamp_fusion.2), kind=kCustom, calls=%fused_computation.5 | custom fusion | bytes 10485840 | tf_op jit(solution)/shard_map/gather | solution.py:75
  138.7 9.4 %fusion.30 = f32[20,128,64]{2,1,0:T(8,128)} fusion(bf16[20,128,2048]{2,1,0:T(8,128)(2,1)} %bitcast.56, bf16[20,64,2048]{2,1,0:T(8,128)(2,1)} %gather_fusion.5), kind=kOutput, calls=%fused_computation.74 | convolution fusion | flops 671088640 | bytes 16384000 | tf_op jit(solution)/shard_map/reshape | solution.py:80
  148.1 17.6 %scatter_custom_fusion = f32[513,64]{1,0:T(8,128)S(1)} fusion(s32[2560]{0:T(1024)S(1)} %fusion.20, f32[2560,64]{1,0:T(8,128)} %bitcast.60, f32[]{:T(128)} %constant.55.clone.1), kind=kCustom, calls=%fused_computation.25 | custom fusion | flops 163840 | bytes 131840 | tf_op jit(solution)/shard_map/scatter-add | solution.py:79
  165.8 0.7 slice.24
  166.5 0.4 reduce-scatter.2.cloned.1.call-start
  167.0 27.1 %fusion.29 = f32[8192,512]{1,0:T(8,128)} fusion(bf16[2048,8192]{1,0:T(8,128)(2,1)} %param.7, bf16[512,2048]{1,0:T(8,128)(2,1)S(1)} %copy-done), kind=kOutput, calls=%fused_computation.73 | convolution fusion | flops 17179869184 | bytes 52428800 | tf_op jit(solution)/shard_map/dot_general | solution.py:93
  194.1 6.4 %fusion.10 = bf16[4,4,64,2048]{3,1,2,0:T(4,128)(2,1)S(1)} fusion(bf16[12,64,2048]{2,1,0:T(8,128)(2,1)} %param.9, s32[4,12]{1,0:T(4,128)S(1)} %copy.41, pred[4,12]{1,0:T(4,128)(4,1)S(1)} %copy.40), kind=kOutput, calls=%fused_computation.19 | convolution fusion | flops 52429184 | bytes 7340272 | tf_op jit(solution)/shard_map/pon,nwa->powa/dot_general | solution.py:40
  200.6 95.5 %all_to_all.10 = bf16[4,4,64,2048]{3,1,2,0:T(4,128)(2,1)S(1)} all-to-all(bf16[4,4,64,2048]{3,1,2,0:T(4,128)(2,1)S(1)} %fusion.10), channel_id=1, replica_groups=mesh['parts'=2,'store'=4,'tensor'=4] {'store'}, dimensions={0} | all-to-all | bytes 8388608 | tf_op jit(solution)/shard_map/all_to_all | solution.py:45
  296.1 4.2 %copy.47 = bf16[4,4,64,2048]{3,2,1,0:T(8,128)(2,1)} copy(bf16[4,4,64,2048]{3,1,2,0:T(4,128)(2,1)S(1)} %all_to_all.10) | data formatting | bytes 8388608 | tf_op jit(solution)/shard_map/all_to_all | solution.py:45
  300.3 6.2 %gather_fusion.7 = bf16[20,64,2048]{2,1,0:T(8,128)(2,1)} fusion(bf16[16,64,2048]{2,1,0:T(8,128)(2,1)} %bitcast.54, s32[1024]{0:T(1024)S(1)} %pad_clamp_fusion.2), kind=kCustom, calls=%fused_computation.7 | custom fusion | bytes 10485840 | tf_op jit(solution)/shard_map/gather | solution.py:85
  306.5 1.0 multiply_convert_fusion
  307.5 5.1 %gather_fusion.6 = bf16[2560,64]{1,0:T(8,128)(2,1)S(1)} fusion(bf16[512,64]{1,0:T(8,128)(2,1)S(1)} %multiply_convert_fusion, s32[3072]{0:T(1024)S(1)} %pad_clamp_fusion), kind=kCustom, calls=%fused_computation.6 | custom fusion | bytes 665600 | tf_op jit(solution)/shard_map/gather | solution.py:84
  312.5 11.1 %fusion.31 = f32[20,128,2048]{2,1,0:T(8,128)} fusion(bf16[20,128,64]{2,1,0:T(8,128)(2,1)S(1)} %bitcast.57, bf16[20,64,2048]{2,1,0:T(8,128)(2,1)} %gather_fusion.7), kind=kOutput, calls=%fused_computation.75 | convolution fusion | flops 671088640 | bytes 26542080 | tf_op jit(solution)/shard_map/bnr,brf->bnf/dot_general | solution.py:86
  323.7 35.6 %scatter_custom_fusion.1 = f32[513,2048]{1,0:T(8,128)} fusion(s32[2560]{0:T(1024)S(1)} %fusion.20, f32[2560,2048]{1,0:T(8,128)} %bitcast.53, f32[]{:T(128)} %constant.55.clone.1), kind=kCustom, calls=%fused_computation.20 | custom fusion | flops 5242880 | bytes 4203008 | tf_op jit(solution)/shard_map/scatter-add | solution.py:87
  359.2 4.6 %slice.25 = f32[512,2048]{1,0:T(8,128)} slice(f32[513,2048]{1,0:T(8,128)} %scatter_custom_fusion.1), slice={[0:512], [0:2048]} | slice | bytes 8388608 | tf_op jit(solution)/shard_map/slice | solution.py:87
  363.8 5.3 %copy.55 = f32[512,2048]{0,1:T(8,128)} copy(f32[512,2048]{1,0:T(8,128)} %slice.25) | data formatting | bytes 8388608
  369.2 5.7 %fusion.4 = bf16[512,2048]{0,1:T(8,128)(2,1)} fusion(f32[512,2048]{0,1:T(8,128)} %copy.55, f32[2048,512]{1,0:T(8,128)} %reduce-scatter.2.cloned.1.call-done), kind=kLoop, calls=%fused_computation.15 | loop fusion | flops 2097152 | bytes 10485760 | tf_op jit(solution)/shard_map/convert_element_type | solution.py:100
  374.9 3.9 %copy.50 = bf16[512,2048]{1,0:T(8,128)(2,1)} copy(bf16[512,2048]{0,1:T(8,128)(2,1)} %fusion.4) | data formatting | bytes 4194304 | tf_op jit(solution)/shard_map/convert_element_type | solution.py:100
  (51 shorter events, 2.5 us)
Async XLA Ops:
  6.5 52.5 %copy-start = (bf16[512,2048]{1,0:T(8,128)(2,1)S(1)}, bf16[512,2048]{1,0:T(8,128)(2,1)}, u32[]{:S(2)}) copy-start(bf16[512,2048]{1,0:T(8,128)(2,1)} %param.6) | copy-start | bytes 6291460
  30.2 5.2 %copy-start.2 = (s32[512]{0:T(512)S(1)}, s32[512]{0:T(512)}, u32[]{:S(2)}) copy-start(s32[512]{0:T(512)} %param.10) | copy-start | bytes 6148
  30.2 5.2 %copy-start.3 = (s32[48]{0:T(128)S(1)}, s32[48]{0:T(128)}, u32[]{:S(2)}) copy-start(s32[48]{0:T(128)} %param.11) | copy-start | bytes 580
  30.2 95.9 %all-to-all-start = ((bf16[4,4,64,2048]{3,1,2,0:T(4,128)(2,1)}), bf16[4,4,64,2048]{3,1,2,0:T(4,128)(2,1)}, u32[]{:S(2)}, u32[]{:S(2)}) async-start(bf16[4,4,64,2048]{3,1,2,0:T(4,128)(2,1)} %fusion.7), calls=%async_computation.1 | async-start | bytes 8388608 | tf_op jit(solution)/shard_map/all_to_all | solution.py:44
  35.2 271.3 %all-reduce.2.cloned.1.call-start = ((), (), s32[]{:S(2)}) async-start(), calls=%async_computation.4 | async-start | bytes 524288 | tf_op jit(solution)/shard_map/psum | solution.py:82
  166.5 202.7 %reduce-scatter.2.cloned.1.call-start = ((), (), s32[]{:S(2)}) async-start(), calls=%async_computation.3 | async-start | bytes 20971520 | tf_op jit(solution)/shard_map/reduce_scatter | solution.py:92
  369.2 9.6 %copy-start.1 = (bf16[512,2048]{1,0:T(8,128)(2,1)S(1)}, bf16[512,2048]{1,0:T(8,128)(2,1)}, u32[]{:S(2)}) copy-start(bf16[512,2048]{1,0:T(8,128)(2,1)} %param.6) | copy-start | bytes 6291460
Sparse Core Ops, SparseCore 0:
  166.6 31.0 all-reduce.1
  200.5 126.1 reduce-scatter.1
where the time goes:
time: 391 us; the launch traced here: 386 us
  blocking collectives  109 us (28%)
  local copies, waits for them, and re-layouts  71.8 us (18%)
  other arithmetic  67.2 us (17%)
  matrix products  62.5 us (16%)
  waiting for transfers between devices  55.6 us (14%)
  between operations  13.7 us (4%)
  starting transfers between devices  5.64 us (1%)
    all_to_all x1, blocking collectives, on_device(): lax.all_to_all(outgoing_up, 'store', split_axis=0, concat_axis=0, tiled=T...  95.5 us
    all_to_all x1, waiting for transfers between devices, on_device(): lax.all_to_all(outgoing_down, 'store', split_axis=0, concat_axis=0, tiled...  55.5 us
    scatter-add x1, other arithmetic, on_device(): jax.ops.segment_sum(block_extra.reshape(block_count * block_rows, hidden_...  35.6 us
    dot_general x1, matrix products, on_device(): lax.dot_general(output_weight, tokens, (((0,), (1,)), ((), ())), preferre...  27.1 us
    scatter-add x1, other arithmetic, on_device(): jax.ops.segment_sum(block_down.reshape(block_count * block_rows, rank_wid...  17.6 us
    gather x1, local copies, waits for them, and re-layouts, on_device(): order[jnp.clip(row_start[block_buffer][:, None] + position, 0, row_count...  15.4 us
    all_gather x1, blocking collectives, on_device(): all_ids = lax.all_gather(row_adapter_index, 'store', axis=0, tiled=True)  13.8 us
    dot_general x1, matrix products, on_device(): jnp.einsum('bnr,brf->bnf', block_low, block_b, preferred_element_type=jnp...  11.1 us
  transfers between devices with their start and end apart: 3, of which 1 were waited for; matrix products, arithmetic and copies ran while one was open for 37% of the time, Pallas kernels for 0%

commit v1 on v0

v1 whole, which is shorter than its diff:
```python
import functools

import jax
import jax.numpy as jnp
from jax import lax
from jax.experimental import pallas as pl
from jax.experimental.pallas import tpu as pltpu
from jax.sharding import PartitionSpec as P

SLOTS = 4
CORES = 2
adapter_scale = 2.0
F32, BF16 = jnp.float32, jnp.bfloat16


def kernel(
    S, T, rank, tile,
    tok_hbm, w_hbm, a_hbm, b_hbm, want_ref, bidx_ref,
    out_ref,
    tok, a_own, b_own, send_a, send_b, got_a, got_b, got_want, want_s,
    wbuf, send1, got1, send2, got2, acc, down, got_down, lowm,
    in_sem, w_sem, want_local,
    want_ss, want_rs, a_ss, a_rs, b_ss, b_rs,
    s1_ss, s1_rs, s2_ss, s2_rs, d_ss, d_rs,
):
    Y = T // CORES
    here = lax.axis_index("store")
    mine = lax.axis_index("tensor")
    my_y, my_c = mine // CORES, mine % CORES
    rows, hidden = out_ref.shape
    width = SLOTS * rank

    def remote(src, dst, ssem, rsem, **where):
        return pltpu.make_async_remote_copy(
            src_ref=src, dst_ref=dst, send_sem=ssem, recv_sem=rsem,
            device_id=where, device_id_type=pl.DeviceIdType.MESH,
        )

    ins = [
        pltpu.make_async_copy(src, dst, in_sem.at[i])
        for i, (src, dst) in enumerate(((a_hbm, a_own), (b_hbm, b_own), (tok_hbm, tok)))
    ]
    for c in ins:
        c.start()

    barrier = pltpu.get_barrier_semaphore()
    for d in range(1, S):
        pl.semaphore_signal(
            barrier, inc=1, device_id={"store": lax.rem(here + d, S)},
            device_id_type=pl.DeviceIdType.MESH,
        )
    for d in range(1, T):
        pl.semaphore_signal(
            barrier, inc=1, device_id={"tensor": lax.rem(mine + d, T)},
            device_id_type=pl.DeviceIdType.MESH,
        )
    pl.semaphore_wait(barrier, S - 1 + T - 1)

    want_copies = []
    for d in range(1, S):
        to = lax.rem(here + d, S)
        c = remote(want_ref.at[to], got_want.at[d], want_ss.at[d], want_rs.at[d], store=to)
        c.start()
        want_copies.append(c)

    per_block = hidden // tile
    tiles = T * per_block

    def weight_copy(i, slot):
        block, sub = i // per_block, i % per_block
        y = lax.rem(my_y + 1 + block % Y, Y)
        core = jnp.where(block < Y, 1 - my_c, my_c)
        col = pl.multiple_of((y * CORES + core) * hidden + sub * tile, tile)
        return pltpu.make_async_copy(w_hbm.at[:, pl.ds(col, tile)], wbuf.at[slot], w_sem.at[slot])

    weight_copy(0, 0).start()

    order = list(range(1, S))
    local = []
    for d in order:
        want_copies[S - d - 1].wait_recv()
        c = pltpu.make_async_copy(got_want.at[S - d], want_s.at[d], want_local.at[d])
        c.start()
        local.append(c)
    c = pltpu.make_async_copy(want_ref.at[here], want_s.at[0], want_local.at[0])
    c.start()
    for x in local + [c]:
        x.wait()

    def fill(own, sends, d):
        for j in range(SLOTS):
            sends[d, j * rank:(j + 1) * rank, :] = own[want_s[d, 0, j]]

    ins[0].wait()
    a_copies, b_copies = {}, {}
    for d in order:
        fill(a_own, send_a, d)
        a_copies[d] = remote(
            send_a.at[d], got_a.at[d], a_ss.at[d], a_rs.at[d], store=lax.rem(here + d, S)
        )
        a_copies[d].start()
    ins[1].wait()
    for d in order:
        fill(b_own, send_b, d)
        b_copies[d] = remote(
            send_b.at[d], got_b.at[d], b_ss.at[d], b_rs.at[d], store=lax.rem(here + d, S)
        )
        b_copies[d].start()
    fill(a_own, send_a, 0)
    fill(b_own, send_b, 0)
    ins[2].wait()

    def product(i):
        slot = lax.rem(i, 2)

        @pl.when(i + 1 < tiles)
        def _():
            weight_copy(i + 1, 1 - slot).start()

        weight_copy(i, slot).wait()
        return jnp.dot(tok[...], wbuf[slot], preferred_element_type=F32)

    def cols(sub):
        return pl.ds(pl.multiple_of(sub * tile, tile), tile)

    s1, s2 = [], []
    for k in range(Y):

        @pl.loop(0, per_block)
        def _(sub, k=k):
            send1[k, :, cols(sub)] = product(k * per_block + sub).astype(BF16)

        c = remote(
            send1.at[k], got1.at[k], s1_ss.at[k], s1_rs.at[k],
            tensor=my_y * CORES + 1 - my_c,
        )
        c.start()
        s1.append(c)
    for k in range(Y):
        s1[k].wait_recv()

        @pl.loop(0, per_block)
        def _(sub, k=k):
            value = product((Y + k) * per_block + sub) + got1[k, :, cols(sub)].astype(F32)
            if k < Y - 1:
                send2[k, :, cols(sub)] = value.astype(BF16)
            else:
                acc[:, cols(sub)] = value

        if k < Y - 1:
            c = remote(
                send2.at[k], got2.at[k], s2_ss.at[k], s2_rs.at[k],
                tensor=lax.rem(my_y + 1 + k, Y) * CORES + my_c,
            )
            c.start()
            s2.append(c)

    bidx = bidx_ref[...]

    def owner_of(d):
        return lax.rem(here + S - d, S)

    total = jnp.zeros((rank, rows), F32)
    for d in range(S):
        if d:
            a_copies[d].wait_recv()
        maps = got_a[d] if d else send_a[0]
        part = lax.dot_general(maps, tok[...], (((1,), (1,)), ((), ())), preferred_element_type=F32)
        for j in range(SLOTS):
            total += jnp.where(
                bidx == owner_of(d) * SLOTS + j, part[j * rank:(j + 1) * rank, :], 0.0
            )
    down[...] = total
    dc = []
    for d in range(1, T):
        c = remote(
            down, got_down.at[d], d_ss.at[d], d_rs.at[d], tensor=lax.rem(mine + d, T)
        )
        c.start()
        dc.append(c)
    for c in s2:
        c.wait_recv()

    @pl.loop(0, per_block)
    def _(sub):
        value = acc[:, cols(sub)]
        for k in range(Y - 1):
            value += got2[k, :, cols(sub)].astype(F32)
        acc[:, cols(sub)] = value

    total = down[...]
    for d in range(1, T):
        dc[d - 1].wait_recv()
        total += got_down[d]
    low = (adapter_scale * total).astype(BF16).astype(F32)
    for d in range(S):
        lifted = jnp.concatenate(
            [jnp.where(bidx == owner_of(d) * SLOTS + j, low, 0.0) for j in range(SLOTS)], axis=0
        )
        lowm[d] = lifted.T.astype(BF16)

    for d in range(S):
        if d:
            b_copies[d].wait_recv()
        maps = got_b.at[d] if d else send_b.at[0]

        @pl.loop(0, per_block)
        def _(sub, d=d, maps=maps):
            value = acc[:, cols(sub)] + jnp.dot(
                lowm[d], maps[:, cols(sub)], preferred_element_type=F32
            )
            if d < S - 1:
                acc[:, cols(sub)] = value
            else:
                out_ref[:, cols(sub)] = value.astype(BF16)

    for c in want_copies + list(a_copies.values()) + list(b_copies.values()) + s1 + s2 + dc:
        c.wait_send()


def on_device(
    S, T,
    tokens, output_weight, adapter_down_maps, adapter_up_maps, row_adapter_index, store_row_index
):
    resident, rank, hidden = adapter_down_maps.shape
    rows = tokens.shape[0]
    count = store_row_index.shape[0]
    Y = T // CORES
    ids = jnp.arange(count, dtype=jnp.int32)

    own_slots = jnp.sum(
        jnp.where(row_adapter_index[None, :] == ids[:, None], store_row_index[:, None], 0), axis=0
    )
    hits = own_slots[None, :] == ids[:, None]
    used = jnp.any(hits, axis=1).astype(jnp.int32)
    earlier = (ids[None, :] < ids[:, None]) & (ids[None, :] // resident == ids[:, None] // resident)
    place = jnp.sum(jnp.where(earlier, used[None, :], 0), axis=1)
    buffer_of = ids // resident * SLOTS + place
    bidx = jnp.sum(jnp.where(hits, buffer_of[:, None], 0), axis=0, keepdims=True)
    lanes = jnp.arange(128, dtype=jnp.int32)
    owners = jnp.arange(S, dtype=jnp.int32)
    match = (
        (used[None, :, None] > 0)
        & (buffer_of[None, :, None] == owners[:, None, None] * SLOTS + lanes[None, None, :])
        & (lanes[None, None, :] < SLOTS)
    )
    want = jnp.sum(jnp.where(match, (ids % resident)[None, :, None], 0), axis=1)
    want = jnp.broadcast_to(want[:, None, :], (S, 8, 128)).astype(jnp.int32)

    width = SLOTS * rank
    tile = min(512, hidden)
    dma = pltpu.SemaphoreType.DMA
    any_, vmem = pl.BlockSpec(memory_space=pl.ANY), pl.BlockSpec(memory_space=pltpu.VMEM)
    flops = 2 * rows * hidden * hidden * T + 4 * rows * width * S * hidden
    return pl.pallas_call(
        functools.partial(kernel, S, T, rank, tile),
        out_shape=jax.ShapeDtypeStruct((rows, hidden), BF16),
        in_specs=[any_] * 4 + [vmem] * 2,
        out_specs=vmem,
        scratch_shapes=[
            pltpu.VMEM((rows, hidden), BF16),
            pltpu.VMEM((resident, rank, hidden), BF16),
            pltpu.VMEM((resident, rank, hidden), BF16),
            pltpu.VMEM((S, width, hidden), BF16),
            pltpu.VMEM((S, width, hidden), BF16),
            pltpu.VMEM((S, width, hidden), BF16),
            pltpu.VMEM((S, width, hidden), BF16),
            pltpu.VMEM((S, 8, 128), jnp.int32),
            pltpu.SMEM((S, 8, 128), jnp.int32),
            pltpu.VMEM((2, hidden, tile), BF16),
            pltpu.VMEM((Y, rows, hidden), BF16),
            pltpu.VMEM((Y, rows, hidden), BF16),
            pltpu.VMEM((max(Y - 1, 1), rows, hidden), BF16),
            pltpu.VMEM((max(Y - 1, 1), rows, hidden), BF16),
            pltpu.VMEM((rows, hidden), F32),
            pltpu.VMEM((rank, rows), F32),
            pltpu.VMEM((T, rank, rows), F32),
            pltpu.VMEM((S, rows, width), BF16),
            dma((3,)), dma((2,)), dma((S,)),
            dma((S,)), dma((S,)), dma((S,)), dma((S,)), dma((S,)), dma((S,)),
            dma((Y,)), dma((Y,)), dma((Y,)), dma((Y,)), dma((T,)), dma((T,)),
        ],
        compiler_params=pltpu.CompilerParams(
            collective_id=0, has_side_effects=True, vmem_limit_bytes=60 * 1024 * 1024
        ),
        cost_estimate=pl.CostEstimate(
            flops=flops, bytes_accessed=2 * hidden * hidden * T, transcendentals=0
        ),
    )(tokens, output_weight, adapter_down_maps, adapter_up_maps, want, bidx)


def solution(mesh):
    placed = (
        P(("parts", "store"), "tensor"),
        P("tensor", None),
        P("store", None, "tensor"),
        P("store", None, "tensor"),
        P(("parts", "store")),
        P("parts"),
    )
    return jax.shard_map(
        functools.partial(on_device, mesh.shape["store"], mesh.shape["tensor"]),
        mesh=mesh,
        in_specs=placed,
        out_specs=P(("parts", "store"), "tensor"),
        check_vma=False,
    )
```

time: 391 us -> 198 us (0.51)
  the two profiles are of different devices: /device:TPU:0 before, /device:TPU:24 now
where the time goes in v1:
time: 198 us
  Pallas kernels  192 us (97%)
  local copies, waits for them, and re-layouts  3.77 us (2%)
  other arithmetic  1.99 us (1%)
    pallas_call x1, Pallas kernels, on_device(): pl.pallas_call(functools.partial(kernel, S, T, rank, tile), out_shape=jax...  192 us

profile of v1, /device:TPU:24, one launch (start us, length us, event | category | flops | bytes accessed | tf_op | source)
XLA Modules:
  0.0 197.5 jit_solution(5263109856803608071)
XLA Ops:
  0.0 0.1 iota_add_fusion
  0.1 0.8 select_reduce_fusion.2
  0.9 0.1 fusion
  1.0 0.2 select_reduce_fusion.3
  1.2 0.1 select_reduce_fusion.1
  1.3 0.7 select_reduce_fusion
  2.0 0.6 broadcast_in_dim.74.want_ref
  2.6 191.7 %shard_map.64 = bf16[512,2048]{1,0:T(8,128)(2,1)} custom-call(bf16[512,2048]{1,0:T(8,128)(2,1)} %tok_hbm.1, bf16[2048,8192]{1,0:T(8,128)(2,1)} %w_hbm.1, bf16[12,64,2048]{2,1,0:T(8,128)(2,1)} %a_hbm.1, bf16[12,64,2048]{2,1,0:T(8,128)(2,1)} %b_hbm.1, s32[4,8,128]{2,1,0:T(8,128)} %broadcast_in_dim.74.want_ref, s32[1,512]{1,0:T(1,128)} %bitcast.1), custom_call_target="tpu_custom_call" | custom-call | flops 21474836480 | bytes 33554432 | tf_op jit(solution)/shard_map/pallas_call | solution.py:255
  194.4 3.2 %copy.8 = bf16[512,2048]{1,0:T(8,128)(2,1)} copy(bf16[512,2048]{1,0:T(8,128)(2,1)} %shard_map.64) | data formatting | bytes 4194304
  (5 shorter events, 0.0 us)

commit v2 on v1

--- a/solution.py
+++ b/solution.py
@@ -9,12 +9,14 @@
 
 SLOTS = 4
 CORES = 2
+CHUNKS = 4
+UP_AFTER = 2
 adapter_scale = 2.0
 F32, BF16 = jnp.float32, jnp.bfloat16
 
 
 def kernel(
-    S, T, rank, tile,
+    S, T, relay, rank, tile,
     tok_hbm, w_hbm, a_hbm, b_hbm, want_ref, bidx_ref,
     out_ref,
     tok, a_own, b_own, send_a, send_b, got_a, got_b, got_want, want_s,
@@ -22,6 +24,7 @@
     in_sem, w_sem, want_local,
     want_ss, want_rs, a_ss, a_rs, b_ss, b_rs,
     s1_ss, s1_rs, s2_ss, s2_rs, d_ss, d_rs,
+    m_ss, m_rs, x_ss, x_rs, f_ss, f_rs, *crossed,
 ):
     Y = T // CORES
     here = lax.axis_index("store")
@@ -54,12 +57,76 @@
             barrier, inc=1, device_id={"tensor": lax.rem(mine + d, T)},
             device_id_type=pl.DeviceIdType.MESH,
         )
-    pl.semaphore_wait(barrier, S - 1 + T - 1)
+    if relay:
+        pl.semaphore_signal(
+            barrier, inc=1, device_id={"parts": 1 - lax.axis_index("parts")},
+            device_id_type=pl.DeviceIdType.MESH,
+        )
+    pl.semaphore_wait(barrier, S - 1 + T - 1 + int(relay))
+
+    if relay:
+        part = lax.axis_index("parts")
+        half = here // 2
+        inner = (here == 1) | (here == 2)
+        nb = here + 1 - 2 * (here % 2)
+        nb_d = lax.rem(nb - here + S, S)
+        far = (2 - half, 3 * (1 - half))
+        share = a_hbm.shape[0] // 2
+        cw = hidden // CHUNKS
+        mine_of = pl.ds(part * share, share)
+        mid, swap, fwd = {}, {}, {}
+        for k in range(2):
+            for h in range(CHUNKS):
+                at, hc = k * CHUNKS + h, pl.ds(h * cw, cw)
+                mid[k, h] = remote(
+                    a_hbm.at[mine_of, :, hc], crossed[at].at[mine_of], m_ss.at[h], m_rs.at[at],
+                    store=2 - half,
+                )
+                swap[k, h] = remote(
+                    crossed[at].at[mine_of], crossed[at].at[mine_of], x_ss.at[at], x_rs.at[at],
+                    parts=1 - part,
+                )
+                fwd[k, h] = remote(
+                    send_a.at[2 + k, :, hc], got_a.at[2 + k, :, hc], f_ss.at[at], f_rs.at[at],
+                    store=nb,
+                )
+
+        @pl.when(inner)
+        def _():
+            for h in range(CHUNKS):
+                mid[0, h].start()
+
+        @pl.when(jnp.logical_not(inner))
+        def _():
+            for h in range(CHUNKS):
+                mid[1, h].start()
+
+    def relay_in(h):
+        @pl.when(inner)
+        def _():
+            for k in range(2):
+                mid[k, h].wait_recv()
+                swap[k, h].start()
+
+    def relay_out(h):
+        @pl.when(inner)
+        def _():
+            for k in range(2):
+                swap[k, h].wait_recv()
+                ref = crossed[k * CHUNKS + h]
+                hs = slice(h * cw, (h + 1) * cw)
+                for j in range(SLOTS):
+                    js = slice(j * rank, (j + 1) * rank)
+                    send_a[2 + k, js, hs] = ref[want_s[nb_d, far[k], j]]
+                fwd[k, h].start()
+                for j in range(SLOTS):
+                    js = slice(j * rank, (j + 1) * rank)
+                    got_a[2 + k, js, hs] = ref[want_s[0, far[k], j]]
 
     want_copies = []
     for d in range(1, S):
         to = lax.rem(here + d, S)
-        c = remote(want_ref.at[to], got_want.at[d], want_ss.at[d], want_rs.at[d], store=to)
+        c = remote(want_ref, got_want.at[d], want_ss.at[d], want_rs.at[d], store=to)
         c.start()
         want_copies.append(c)
 
@@ -82,33 +149,59 @@
         c = pltpu.make_async_copy(got_want.at[S - d], want_s.at[d], want_local.at[d])
         c.start()
         local.append(c)
-    c = pltpu.make_async_copy(want_ref.at[here], want_s.at[0], want_local.at[0])
+    c = pltpu.make_async_copy(want_ref, want_s.at[0], want_local.at[0])
     c.start()
     for x in local + [c]:
         x.wait()
 
-    def fill(own, sends, d):
+    def fill(own, sends, d, at=None):
         for j in range(SLOTS):
-            sends[d, j * rank:(j + 1) * rank, :] = own[want_s[d, 0, j]]
+            sends[d if at is None else at, j * rank:(j + 1) * rank, :] = own[want_s[d, here, j]]
 
     ins[0].wait()
     a_copies, b_copies = {}, {}
-    for d in order:
-        fill(a_own, send_a, d)
-        a_copies[d] = remote(
-            send_a.at[d], got_a.at[d], a_ss.at[d], a_rs.at[d], store=lax.rem(here + d, S)
-        )
-        a_copies[d].start()
-    ins[1].wait()
-    for d in order:
-        fill(b_own, send_b, d)
-        b_copies[d] = remote(
-            send_b.at[d], got_b.at[d], b_ss.at[d], b_rs.at[d], store=lax.rem(here + d, S)
-        )
-        b_copies[d].start()
+    if relay:
+        fill(a_own, send_a, nb_d, 1)
+        a_copies[1] = remote(send_a.at[1], got_a.at[1], a_ss.at[1], a_rs.at[1], store=nb)
+        a_copies[1].start()
+    else:
+        for d in order:
+            fill(a_own, send_a, d)
+            a_copies[d] = remote(
+                send_a.at[d], got_a.at[d], a_ss.at[d], a_rs.at[d], store=lax.rem(here + d, S)
+            )
+            a_copies[d].start()
+
+    def send_up():
+        ins[1].wait()
+        for d in order:
+            fill(b_own, send_b, d)
+            b_copies[d] = remote(
+                send_b.at[d], got_b.at[d], b_ss.at[d], b_rs.at[d], store=lax.rem(here + d, S)
+            )
+            b_copies[d].start()
+        fill(b_own, send_b, 0)
+
+    if not relay:
+        send_up()
     fill(a_own, send_a, 0)
-    fill(b_own, send_b, 0)
     ins[2].wait()
+
+    steps = []
+    if relay:
+        for h in range(CHUNKS):
+            steps.append(functools.partial(relay_in, h))
+            if h:
+                steps.append(functools.partial(relay_out, h - 1))
+            if h == UP_AFTER:
+                steps.append(send_up)
+        steps.append(functools.partial(relay_out, CHUNKS - 1))
+    steps_per_block = 2
+
+    def some_steps(last=False):
+        for step in steps[:None if last else steps_per_block]:
+            step()
+        del steps[:None if last else steps_per_block]
 
     def product(i):
         slot = lax.rem(i, 2)
@@ -136,6 +229,7 @@
         )
         c.start()
         s1.append(c)
+        some_steps()
     for k in range(Y):
         s1[k].wait_recv()
 
@@ -154,6 +248,7 @@
             )
             c.start()
             s2.append(c)
+        some_steps(k == Y - 1)
 
     bidx = bidx_ref[...]
 
@@ -162,13 +257,23 @@
 
     total = jnp.zeros((rank, rows), F32)
     for d in range(S):
-        if d:
+        owner = owner_of(d)
+        if relay and d:
+            owner = (nb, *far)[d - 1]
+        if d and d in a_copies:
             a_copies[d].wait_recv()
+        elif d:
+
+            @pl.when(jnp.logical_not(inner))
+            def _(d=d):
+                for h in range(CHUNKS):
+                    fwd[d - 2, h].wait_recv()
+
         maps = got_a[d] if d else send_a[0]
-        part = lax.dot_general(maps, tok[...], (((1,), (1,)), ((), ())), preferred_element_type=F32)
+        piece = lax.dot_general(maps, tok[...], (((1,), (1,)), ((), ())), preferred_element_type=F32)
         for j in range(SLOTS):
             total += jnp.where(
-                bidx == owner_of(d) * SLOTS + j, part[j * rank:(j + 1) * rank, :], 0.0
+                bidx == owner * SLOTS + j, piece[j * rank:(j + 1) * rank, :], 0.0
             )
     down[...] = total
     dc = []
@@ -216,10 +321,18 @@
 
     for c in want_copies + list(a_copies.values()) + list(b_copies.values()) + s1 + s2 + dc:
         c.wait_send()
+    if relay:
+        for h in range(CHUNKS):
+            mid[0, h].wait_send()
+
+        @pl.when(inner)
+        def _():
+            for c in list(swap.values()) + list(fwd.values()):
+                c.wait_send()
 
 
 def on_device(
-    S, T,
+    S, T, parts,
     tokens, output_weight, adapter_down_maps, adapter_up_maps, row_adapter_index, store_row_index
 ):
     resident, rank, hidden = adapter_down_maps.shape
@@ -245,15 +358,19 @@
         & (lanes[None, None, :] < SLOTS)
     )
     want = jnp.sum(jnp.where(match, (ids % resident)[None, :, None], 0), axis=1)
-    want = jnp.broadcast_to(want[:, None, :], (S, 8, 128)).astype(jnp.int32)
+    table = -(-S // 8) * 8
+    want = jnp.pad(want, ((0, table - S), (0, 0))).astype(jnp.int32)
 
     width = SLOTS * rank
     tile = min(512, hidden)
+    relay = S == 4 and parts == 2 and resident % 2 == 0 and hidden % (128 * CHUNKS) == 0
+    both = 2 * CHUNKS
+    crossed = [pltpu.VMEM((resident, rank, hidden // CHUNKS), BF16)] * (both if relay else 0)
     dma = pltpu.SemaphoreType.DMA
     any_, vmem = pl.BlockSpec(memory_space=pl.ANY), pl.BlockSpec(memory_space=pltpu.VMEM)
     flops = 2 * rows * hidden * hidden * T + 4 * rows * width * S * hidden
     return pl.pallas_call(
-        functools.partial(kernel, S, T, rank, tile),
+        functools.partial(kernel, S, T, relay, rank, tile),
         out_shape=jax.ShapeDtypeStruct((rows, hidden), BF16),
         in_specs=[any_] * 4 + [vmem] * 2,
         out_specs=vmem,
@@ -265,8 +382,8 @@
             pltpu.VMEM((S, width, hidden), BF16),
             pltpu.VMEM((S, width, hidden), BF16),
             pltpu.VMEM((S, width, hidden), BF16),
-            pltpu.VMEM((S, 8, 128), jnp.int32),
-            pltpu.SMEM((S, 8, 128), jnp.int32),
+            pltpu.VMEM((S, table, 128), jnp.int32),
+            pltpu.SMEM((S, table, 128), jnp.int32),
             pltpu.VMEM((2, hidden, tile), BF16),
             pltpu.VMEM((Y, rows, hidden), BF16),
             pltpu.VMEM((Y, rows, hidden), BF16),
@@ -279,6 +396,8 @@
             dma((3,)), dma((2,)), dma((S,)),
             dma((S,)), dma((S,)), dma((S,)), dma((S,)), dma((S,)), dma((S,)),
             dma((Y,)), dma((Y,)), dma((Y,)), dma((Y,)), dma((T,)), dma((T,)),
+            dma((CHUNKS,)), dma((both,)), dma((both,)), dma((both,)), dma((both,)), dma((both,)),
+            *crossed,
         ],
         compiler_params=pltpu.CompilerParams(
             collective_id=0, has_side_effects=True, vmem_limit_bytes=60 * 1024 * 1024
@@ -299,7 +418,7 @@
         P("parts"),
     )
     return jax.shard_map(
-        functools.partial(on_device, mesh.shape["store"], mesh.shape["tensor"]),
+        functools.partial(on_device, mesh.shape["store"], mesh.shape["tensor"], mesh.shape["parts"]),
         mesh=mesh,
         in_specs=placed,
         out_specs=P(("parts", "store"), "tensor"),

time: 198 us -> 231 us (1.17)
  the two profiles are of different devices: /device:TPU:24 before, /device:TPU:0 now
where the time goes in v2:
time: 231 us; the launch traced here: 230 us
  Pallas kernels  224 us (97%)
  local copies, waits for them, and re-layouts  3.76 us (2%)
    pallas_call x1, Pallas kernels, on_device(): pl.pallas_call(functools.partial(kernel, S, T, relay, rank, tile), out_sh...  224 us

profile of v2, /device:TPU:0, one launch (start us, length us, event | category | flops | bytes accessed | tf_op | source)
XLA Modules:
  0.0 229.8 jit_solution(6937675062407489589)
XLA Ops:
  0.0 0.1 iota_add_fusion
  0.1 0.8 select_reduce_fusion.2
  0.9 0.1 fusion
  1.0 0.2 select_reduce_fusion.3
  1.2 0.1 select_reduce_fusion.1
  1.3 0.7 select_reduce_fusion
  2.0 0.6 pad.4.want_ref
  2.6 224.1 %shard_map.64 = bf16[512,2048]{1,0:T(8,128)(2,1)} custom-call(bf16[512,2048]{1,0:T(8,128)(2,1)} %tok_hbm.1, bf16[2048,8192]{1,0:T(8,128)(2,1)} %w_hbm.1, bf16[12,64,2048]{2,1,0:T(8,128)(2,1)} %a_hbm.1, bf16[12,64,2048]{2,1,0:T(8,128)(2,1)} %b_hbm.1, s32[8,128]{1,0:T(8,128)} %pad.4.want_ref, s32[1,512]{1,0:T(1,128)} %bitcast.1), custom_call_target="tpu_custom_call" | custom-call | flops 21474836480 | bytes 33554432 | tf_op jit(solution)/shard_map/pallas_call | solution.py:372
  226.7 3.2 %copy.8 = bf16[512,2048]{1,0:T(8,128)(2,1)} copy(bf16[512,2048]{1,0:T(8,128)(2,1)} %shard_map.64) | data formatting | bytes 4194304
  (5 shorter events, 0.0 us)

commit v3 on v1

--- a/solution.py
+++ b/solution.py
@@ -22,6 +22,7 @@
     in_sem, w_sem, want_local,
     want_ss, want_rs, a_ss, a_rs, b_ss, b_rs,
     s1_ss, s1_rs, s2_ss, s2_rs, d_ss, d_rs,
+    relay_a, relay_b, r_ss, r_rs, g_ss, g_rs,
 ):
     Y = T // CORES
     here = lax.axis_index("store")
@@ -87,25 +88,46 @@
     for x in local + [c]:
         x.wait()
 
+    hops, ons = [], []
+    if S == 4:
+        back, top = lax.rem(here + 3, 4), pl.ds(width // 2, width // 2)
+        for i, (a, r, g) in enumerate(((send_a, relay_a, got_a), (send_b, relay_b, got_b))):
+            hops.append(remote(a.at[2, top], r, r_ss.at[i], r_rs.at[i], store=back))
+            ons.append(remote(r, g.at[2, top], g_ss.at[i], g_rs.at[i], store=back))
+
+    def pass_on(i):
+        if hops:
+            hops[i].wait_recv()
+            ons[i].start()
+
     def fill(own, sends, d):
         for j in range(SLOTS):
             sends[d, j * rank:(j + 1) * rank, :] = own[want_s[d, 0, j]]
+
+    def part_of(d):
+        return pl.ds(0, width // 2 if hops and d == 2 else width)
 
     ins[0].wait()
     a_copies, b_copies = {}, {}
     for d in order:
         fill(a_own, send_a, d)
         a_copies[d] = remote(
-            send_a.at[d], got_a.at[d], a_ss.at[d], a_rs.at[d], store=lax.rem(here + d, S)
+            send_a.at[d, part_of(d)], got_a.at[d, part_of(d)], a_ss.at[d], a_rs.at[d],
+            store=lax.rem(here + d, S),
         )
         a_copies[d].start()
+        if hops and d == 2:
+            hops[0].start()
     ins[1].wait()
     for d in order:
         fill(b_own, send_b, d)
         b_copies[d] = remote(
-            send_b.at[d], got_b.at[d], b_ss.at[d], b_rs.at[d], store=lax.rem(here + d, S)
+            send_b.at[d, part_of(d)], got_b.at[d, part_of(d)], b_ss.at[d], b_rs.at[d],
+            store=lax.rem(here + d, S),
         )
         b_copies[d].start()
+        if hops and d == 2:
+            hops[1].start()
     fill(a_own, send_a, 0)
     fill(b_own, send_b, 0)
     ins[2].wait()
@@ -136,6 +158,7 @@
         )
         c.start()
         s1.append(c)
+    pass_on(0)
     for k in range(Y):
         s1[k].wait_recv()
 
@@ -164,6 +187,8 @@
     for d in range(S):
         if d:
             a_copies[d].wait_recv()
+            if hops and d == 2:
+                ons[0].wait_recv()
         maps = got_a[d] if d else send_a[0]
         part = lax.dot_general(maps, tok[...], (((1,), (1,)), ((), ())), preferred_element_type=F32)
         for j in range(SLOTS):
@@ -178,6 +203,7 @@
         )
         c.start()
         dc.append(c)
+    pass_on(1)
     for c in s2:
         c.wait_recv()
 
@@ -202,6 +228,8 @@
     for d in range(S):
         if d:
             b_copies[d].wait_recv()
+            if hops and d == 2:
+                ons[1].wait_recv()
         maps = got_b.at[d] if d else send_b.at[0]
 
         @pl.loop(0, per_block)
@@ -214,7 +242,7 @@
             else:
                 out_ref[:, cols(sub)] = value.astype(BF16)
 
-    for c in want_copies + list(a_copies.values()) + list(b_copies.values()) + s1 + s2 + dc:
+    for c in want_copies + list(a_copies.values()) + list(b_copies.values()) + s1 + s2 + dc + hops + ons:
         c.wait_send()
 
 
@@ -279,6 +307,9 @@
             dma((3,)), dma((2,)), dma((S,)),
             dma((S,)), dma((S,)), dma((S,)), dma((S,)), dma((S,)), dma((S,)),
             dma((Y,)), dma((Y,)), dma((Y,)), dma((Y,)), dma((T,)), dma((T,)),
+            pltpu.VMEM((width // 2, hidden), BF16),
+            pltpu.VMEM((width // 2, hidden), BF16),
+            dma((2,)), dma((2,)), dma((2,)), dma((2,)),
         ],
         compiler_params=pltpu.CompilerParams(
             collective_id=0, has_side_effects=True, vmem_limit_bytes=60 * 1024 * 1024

time: 198 us -> 203 us (1.025)
  the two profiles are of different devices: /device:TPU:24 before, /device:TPU:0 now
where the time goes in v3:
time: 203 us
  Pallas kernels  197 us (97%)
  local copies, waits for them, and re-layouts  3.77 us (2%)
    pallas_call x1, Pallas kernels, on_device(): pl.pallas_call(functools.partial(kernel, S, T, rank, tile), out_shape=jax...  197 us

profile of v3, /device:TPU:0, one launch (start us, length us, event | category | flops | bytes accessed | tf_op | source)
XLA Modules:
  0.0 202.6 jit_solution(6060169013543154482)
XLA Ops:
  0.0 0.1 iota_add_fusion
  0.1 0.8 select_reduce_fusion.2
  0.9 0.1 fusion
  1.0 0.2 select_reduce_fusion.3
  1.2 0.1 select_reduce_fusion.1
  1.3 0.7 select_reduce_fusion
  2.0 0.6 broadcast_in_dim.74.want_ref
  2.6 196.9 %shard_map.64 = bf16[512,2048]{1,0:T(8,128)(2,1)} custom-call(bf16[512,2048]{1,0:T(8,128)(2,1)} %tok_hbm.1, bf16[2048,8192]{1,0:T(8,128)(2,1)} %w_hbm.1, bf16[12,64,2048]{2,1,0:T(8,128)(2,1)} %a_hbm.1, bf16[12,64,2048]{2,1,0:T(8,128)(2,1)} %b_hbm.1, s32[4,8,128]{2,1,0:T(8,128)} %broadcast_in_dim.74.want_ref, s32[1,512]{1,0:T(1,128)} %bitcast.1), custom_call_target="tpu_custom_call" | custom-call | flops 21474836480 | bytes 33554432 | tf_op jit(solution)/shard_map/pallas_call | solution.py:283
  199.5 3.2 %copy.8 = bf16[512,2048]{1,0:T(8,128)(2,1)} copy(bf16[512,2048]{1,0:T(8,128)(2,1)} %shard_map.64) | data formatting | bytes 4194304
  (5 shorter events, 0.0 us)
